TPU v7x, 32 devices: a whole 2x2x4 slice. The times are simulated.
32 devices in a mesh: ens: 2 (over x), dom: 8 (over z, y), lat: 2 (over core).
Axes of the slice: x: 2, y: 2, z: 4, core: 2. Of those that a mesh axis runs over, the one named last changes fastest.
Arguments:
- node_lat: bfloat16 [5120, 512], P(('ens', 'dom'), 'lat'), parts along dimension 0, may hold values from -6 to 6
- edge_lat: bfloat16 [40960, 512], P(('ens', 'dom'), 'lat'), parts along dimension 0, may hold values from -6 to 6
- halo_rows: int32 [16, 8, 80], P('ens'), parts along dimension 0, may hold values from 0 to 320, as said below
- edge_sender: int32 [40960], P(('ens', 'dom')), parts along dimension 0, may hold values from 0 to 959, as said below
- edge_receiver: int32 [40960], P(('ens', 'dom')), parts along dimension 0, may hold values from 0 to 319, as said below
- edge_w_in: bfloat16 [1536, 512], replicated, may hold values from -0.15625 to 0.15625
- edge_b_in: float32 [512], replicated, may hold values from -3 to 3
- edge_w_out: bfloat16 [512, 512], replicated, may hold values from -0.25 to 0.25
- edge_b_out: float32 [512], replicated, may hold values from -4 to 4
- edge_gain: float32 [512], replicated, may hold values from 0.1 to 1.9
- edge_shift: float32 [512], replicated, may hold values from -3 to 3
- node_w_in: bfloat16 [1024, 512], replicated, may hold values from -0.1875 to 0.1875
- node_b_in: float32 [512], replicated, may hold values from -3 to 3
- node_w_out: bfloat16 [512, 512], replicated, may hold values from -0.25 to 0.25
- node_b_out: float32 [512], replicated, may hold values from -4 to 4
- node_gain: float32 [512], replicated, may hold values from 0.1 to 1.9
- node_shift: float32 [512], replicated, may hold values from -3 to 3
- node_ct: bfloat16 [5120, 512], P(('ens', 'dom'), 'lat'), parts along dimension 0, may hold values from -6 to 6
- edge_ct: bfloat16 [40960, 512], P(('ens', 'dom'), 'lat'), parts along dimension 0, may hold values from -6 to 6
Outputs:
- node_new: bfloat16 [5120, 512], P(('ens', 'dom'), 'lat'), parts along dimension 0
- edge_new: bfloat16 [40960, 512], P(('ens', 'dom'), 'lat'), parts along dimension 0
- node_grad: float32 [5120, 512], P(('ens', 'dom'), 'lat'), parts along dimension 0
- edge_grad: float32 [40960, 512], P(('ens', 'dom'), 'lat'), parts along dimension 0
There are 2 independent parts, one for each index of `ens`. A program takes and returns all parts, laid end to end along the dimension named above; an argument that names none is the same for every part. Nothing has to cross between parts.
Inputs may be any that keep to these rules, and one draw needn't show every extreme that they name: halo_rows[p, q] lists distinct rows of partition p read by edges of partition q: its used slots come first, and every empty slot holds 320. The list of a partition to itself is empty, every other list holds one or more rows, and the list of p to p + 1 (cyclically) is full. `edge_sender`: A value s below 320 is a row of the edge's own partition p; otherwise s = 320 + q * 80 + k names used slot k of halo_rows[q, p]. `edge_receiver`: the edges of a partition fall into 2 aligned blocks of 1280 rows, and the receivers of block j are rows j * 160 to (j + 1) * 160 - 1.
All inputs are finite; a program needn't handle non-finite values.
Results may differ from a plain program's by a relative error of at most 0.012.
Values may be sent and summed in bfloat16 or wider, within the bound.
A program may use at most 64 MiB of HBM per device.

v0:
```python
import jax
import jax.numpy as jnp
from jax import lax
from jax.sharding import PartitionSpec as P


def finish_block(before, w_out, b_out, scales, offsets):
    active = jax.nn.silu(before).astype(jnp.bfloat16)
    output = jnp.dot(active, w_out, preferred_element_type=jnp.float32) + b_out
    average = jnp.mean(output, axis=-1, keepdims=True)
    centred = output - average
    variance = jnp.mean(centred * centred, axis=-1, keepdims=True)
    return centred * lax.rsqrt(variance + 1e-05) * scales + offsets


def process(edge_full, sender_bf, node_full, receiver, edge_params, node_params):
    width = node_full.shape[1]
    w_edge = edge_params[0]
    receiver_bf = jnp.take(node_full, receiver, axis=0).astype(jnp.bfloat16)
    before = jnp.dot(
        edge_full.astype(jnp.bfloat16), w_edge[:width], preferred_element_type=jnp.float32
    )
    before = before + jnp.dot(
        sender_bf, w_edge[width : 2 * width], preferred_element_type=jnp.float32
    )
    before = before + jnp.dot(receiver_bf, w_edge[2 * width :], preferred_element_type=jnp.float32)
    before = before + edge_params[1]
    edge_new = (
        edge_full
        + finish_block(before, edge_params[2], edge_params[3], edge_params[4], edge_params[5])
    ).astype(jnp.bfloat16)
    summed = jax.ops.segment_sum(
        edge_new.astype(jnp.float32), receiver, num_segments=node_full.shape[0]
    )
    w_node = node_params[0]
    node_before = jnp.dot(
        node_full.astype(jnp.bfloat16), w_node[:width], preferred_element_type=jnp.float32
    )
    node_before = node_before + jnp.dot(
        summed.astype(jnp.bfloat16), w_node[width:], preferred_element_type=jnp.float32
    )
    node_before = node_before + node_params[1]
    node_new = (
        node_full
        + finish_block(node_before, node_params[2], node_params[3], node_params[4], node_params[5])
    ).astype(jnp.bfloat16)
    return (edge_new, node_new)


def on_device(
    node_lat,
    edge_lat,
    halo_rows,
    edge_sender,
    edge_receiver,
    edge_w_in,
    edge_b_in,
    edge_w_out,
    edge_b_out,
    edge_gain,
    edge_shift,
    node_w_in,
    node_b_in,
    node_w_out,
    node_b_out,
    node_gain,
    node_shift,
    node_ct,
    edge_ct,
):
    edge_params = (edge_w_in, edge_b_in, edge_w_out, edge_b_out, edge_gain, edge_shift)
    node_params = (node_w_in, node_b_in, node_w_out, node_b_out, node_gain, node_shift)
    member = lax.axis_index("dom")
    domains = lax.axis_size("dom")
    halves = lax.axis_size("lat")
    lat_index = lax.axis_index("lat")
    node_rows, features = node_lat.shape
    edge_rows = edge_lat.shape[0]
    slot_count = halo_rows.shape[2]
    everyone = lax.all_gather(node_lat, "dom", axis=0, tiled=True)
    direct = edge_sender < node_rows
    offset = jnp.maximum(edge_sender - node_rows, 0)
    source = offset // slot_count
    remote = halo_rows[source, member, offset % slot_count]
    global_row = jnp.where(direct, member * node_rows + edge_sender, source * node_rows + remote)
    sender_rows = jnp.take(everyone, global_row, axis=0)
    edge_whole, sender_whole, edge_cot, node_whole, node_cot = (
        lax.all_to_all(edge_lat, "lat", split_axis=0, concat_axis=1, tiled=True),
        lax.all_to_all(sender_rows, "lat", split_axis=0, concat_axis=1, tiled=True),
        lax.all_to_all(edge_ct, "lat", split_axis=0, concat_axis=1, tiled=True),
        lax.all_to_all(node_lat, "lat", split_axis=0, concat_axis=1, tiled=True),
        lax.all_to_all(node_ct, "lat", split_axis=0, concat_axis=1, tiled=True),
    )
    edge_block = edge_rows // halves
    node_block = node_rows // halves
    receiver = (
        lax.dynamic_slice_in_dim(edge_receiver, lat_index * edge_block, edge_block)
        - lat_index * node_block
    )

    def forward(node_full, edge_full, sender_bf):
        return process(edge_full, sender_bf, node_full, receiver, edge_params, node_params)

    outputs, pullback = jax.vjp(
        forward, node_whole.astype(jnp.float32), edge_whole.astype(jnp.float32), sender_whole
    )
    edge_new, node_new = outputs
    node_grad, edge_grad, sender_grad = pullback((edge_cot, node_cot))
    edge_out, node_out, sender_back = (
        lax.all_to_all(edge_new, "lat", split_axis=1, concat_axis=0, tiled=True),
        lax.all_to_all(node_new, "lat", split_axis=1, concat_axis=0, tiled=True),
        lax.all_to_all(sender_grad, "lat", split_axis=1, concat_axis=0, tiled=True),
    )
    edge_back, node_back = (
        lax.all_to_all(edge_grad, "lat", split_axis=1, concat_axis=0, tiled=True),
        lax.all_to_all(node_grad, "lat", split_axis=1, concat_axis=0, tiled=True),
    )
    sender_sums = sender_back.astype(jnp.float32)
    node_total = node_back
    spread = jax.ops.segment_sum(sender_sums, global_row, num_segments=domains * node_rows)
    node_total = node_total + lax.psum_scatter(
        spread.astype(jnp.bfloat16), "dom", scatter_dimension=0, tiled=True
    ).astype(jnp.float32)
    return (node_out, edge_out, node_total, edge_back)


def solution(mesh):
    placed = (
        P(("ens", "dom"), "lat"),
        P(("ens", "dom"), "lat"),
        P("ens", None, None),
        P(("ens", "dom")),
        P(("ens", "dom")),
        P(),
        P(),
        P(),
        P(),
        P(),
        P(),
        P(),
        P(),
        P(),
        P(),
        P(),
        P(),
        P(("ens", "dom"), "lat"),
        P(("ens", "dom"), "lat"),
    )
    return jax.shard_map(
        on_device,
        mesh=mesh,
        in_specs=placed,
        out_specs=(
            P(("ens", "dom"), "lat"),
            P(("ens", "dom"), "lat"),
            P(("ens", "dom"), "lat"),
            P(("ens", "dom"), "lat"),
        ),
        check_vma=False,
    )
```

profile of v0, /device:TPU:26, one launch (start us, length us, event | category | flops | bytes accessed | tf_op | source)
XLA Modules:
  0.0 222.6 jit_solution(13720177386217007659)
XLA Ops:
  7.2 3.6 %all-to-all-start.5 = ((bf16[2,160,256]{2,1,0:T(8,128)(2,1)}), bf16[2,160,256]{2,1,0:T(8,128)(2,1)S(1)}, u32[]{:S(2)}, u32[]{:S(2)}) async-start(bf16[2,160,256]{2,1,0:T(8,128)(2,1)} %bitcast.86), calls=%async_computation.5 | async-start | bytes 327680 | tf_op jit(solution)/shard_map/all_to_all | solution.py:92
  12.2 3.4 %all-to-all-start = ((bf16[2,160,256]{2,1,0:T(8,128)(2,1)}), bf16[2,160,256]{2,1,0:T(8,128)(2,1)S(1)}, u32[]{:S(2)}, u32[]{:S(2)}) async-start(bf16[2,160,256]{2,1,0:T(8,128)(2,1)} %bitcast.82), calls=%async_computation | async-start | bytes 327680 | tf_op jit(solution)/shard_map/all_to_all | solution.py:91
  17.9 3.6 %all-to-all-start.1 = ((bf16[2,1280,256]{1,2,0:T(8,128)(2,1)}), bf16[2,1280,256]{1,2,0:T(8,128)(2,1)S(1)}, u32[]{:S(2)}, u32[]{:S(2)}) async-start(bf16[2,1280,256]{1,2,0:T(8,128)(2,1)} %copy.46), calls=%async_computation.1 | async-start | bytes 2621440 | tf_op jit(solution)/shard_map/all_to_all | solution.py:88
  21.6 14.4 %gather_fusion = s32[2560]{0:T(1024)S(1)} fusion(s32[8,8,80]{2,1,0:T(8,128)S(1)} %copy-done.2, s32[2560]{0:T(1024)S(1)} %fusion.45), kind=kCustom, calls=%fused_computation | custom fusion | bytes 51200 | tf_op jit(solution)/shard_map/gather | solution.py:84
  37.7 4.7 %gather_fusion.2 = bf16[1280,512]{1,0:T(8,128)(2,1)} fusion(bf16[160,512]{1,0:T(8,128)(2,1)S(1)} %bitcast.62, s32[2048]{0:T(1024)S(1)} %pad_clamp_fusion.2), kind=kCustom, calls=%fused_computation.2 | custom fusion | bytes 2626560 | tf_op jit(solution)/shard_map/jvp(jit(_take))/gather | solution.py:19
  46.9 8.5 %all-gather.2.cloned.1.call-done = bf16[2560,256]{1,0:T(8,128)(2,1)} async-done(((bf16[320,256]{1,0:T(8,128)(2,1)}), bf16[2560,256]{1,0:T(8,128)(2,1)}) %all-gather.2.cloned.1.call-update) | async-done | bytes 1310736 | tf_op jit(solution)/shard_map/all_gather | solution.py:80
  55.3 8.3 %gather_fusion.1 = bf16[2560,256]{1,0:T(8,128)(2,1)} fusion(bf16[2560,256]{1,0:T(8,128)(2,1)} %all-gather.2.cloned.1.call-done, s32[3072]{0:T(1024)S(1)} %pad_clamp_fusion), kind=kCustom, calls=%fused_computation.1 | custom fusion | bytes 2631680 | tf_op jit(solution)/shard_map/jit(_take)/gather | solution.py:86
  67.5 5.6 %all_to_all.175 = bf16[2,1280,256]{1,2,0:T(8,128)(2,1)} all-to-all(bf16[2,1280,256]{1,2,0:T(8,128)(2,1)S(1)} %broadcast_select_fusion), channel_id=1, replica_groups=mesh['ens'=2,'dom'=8,'lat'=2] {'lat'}, dimensions={0} | all-to-all | bytes 2621440 | tf_op jit(solution)/shard_map/all_to_all | solution.py:89
  73.1 4.5 %all-to-all-start.6 = ((bf16[2,1280,256]{1,2,0:T(8,128)(2,1)}), bf16[2,1280,256]{1,2,0:T(8,128)(2,1)}, u32[]{:S(2)}, u32[]{:S(2)}) async-start(bf16[2,1280,256]{1,2,0:T(8,128)(2,1)} %copy.52), calls=%async_computation.6 | async-start | bytes 2621440 | tf_op jit(solution)/shard_map/all_to_all | solution.py:90
  87.8 2.8 %copy.48 = f32[1280,512]{1,0:T(8,128)} copy(bf16[1280,512]{0,1:T(8,128)(2,1)} %add_convert_fusion) | data formatting | bytes 3932160 | tf_op jit(solution)/shard_map/jvp()/convert_element_type | solution.py:33
  90.6 11.0 %scatter_custom_fusion = f32[160,512]{1,0:T(8,128)} fusion(s32[1280]{0:T(1024)S(1)} %get-tuple-element.9, f32[1280,512]{1,0:T(8,128)} %copy.48, f32[]{:T(128)} %constant.42.clone.1), kind=kCustom, calls=%fused_computation.84 | custom fusion | flops 655360 | bytes 328192 | tf_op jit(solution)/shard_map/jvp()/scatter-add | solution.py:32
  106.6 4.7 %gather_fusion.3 = bf16[1280,512]{1,0:T(8,128)(2,1)} fusion(bf16[160,512]{1,0:T(8,128)(2,1)S(1)} %fusion.17, s32[2048]{0:T(1024)S(1)} %pad_clamp_fusion.1), kind=kCustom, calls=%fused_computation.3 | custom fusion | bytes 2626560 | tf_op jit(solution)/shard_map/transpose(jvp())/gather | solution.py:32
  111.3 2.4 %copy.53 = bf16[1280,512]{0,1:T(8,128)(2,1)} copy(bf16[1280,512]{1,0:T(8,128)(2,1)} %gather_fusion.3) | data formatting | bytes 2621440 | tf_op jit(solution)/shard_map/transpose(jvp())/gather | solution.py:32
  113.7 2.5 %fusion.5 = (f32[1280]{0:T(1024)S(1)}, bf16[1280,512]{0,1:T(8,128)(2,1)S(1)}) fusion(f32[1280,512]{0,1:T(8,128)S(1)} %get-tuple-element.18, f32[512]{0:T(512)S(1)} %copy-done.23, f32[1280]{0:T(1024)S(1)} %broadcast_multiply_fusion, bf16[1280,512]{0,1:T(8,128)(2,1)} %copy.53, pred[1280]{0:T(1024)(128)(4,1)S(1)} %get-tuple-element.8, ...), kind=kLoop, calls=%fused_computation.25 | loop fusion | flops 6552320 | bytes 6567168 | tf_op jit(solution)/shard_map/transpose(jvp())/reduce_sum | solution.py:13
  122.6 4.8 %all_to_all.176 = bf16[1280,2,256]{0,2,1:T(8,128)(2,1)S(1)} all-to-all(bf16[1280,2,256]{0,2,1:T(8,128)(2,1)S(1)} %bitcast.80), channel_id=1, replica_groups=mesh['ens'=2,'dom'=8,'lat'=2] {'lat'}, dimensions={1} | all-to-all | bytes 2621440 | tf_op jit(solution)/shard_map/all_to_all | solution.py:112
  129.7 16.3 %scatter_custom_fusion.2 = f32[2560,256]{1,0:T(8,128)} fusion(s32[2560]{0:T(1024)S(1)} %get-tuple-element.13, f32[2560,256]{1,0:T(8,128)} %bitcast.76, f32[]{:T(128)} %constant.42.clone.1), kind=kCustom, calls=%fused_computation.37 | custom fusion | flops 655360 | bytes 2621952 | tf_op jit(solution)/shard_map/scatter-add | solution.py:120
  146.0 3.1 %convert_element_type.126 = bf16[2560,256]{1,0:T(8,128)(2,1)} convert(f32[2560,256]{1,0:T(8,128)} %scatter_custom_fusion.2) | non-fusion elementwise | flops 655360 | bytes 3932160 | tf_op jit(solution)/shard_map/convert_element_type | solution.py:122
  149.1 4.6 %all_to_all.177 = bf16[160,2,256]{2,0,1:T(8,128)(2,1)} all-to-all(bf16[160,2,256]{2,0,1:T(8,128)(2,1)S(1)} %bitcast.85), channel_id=1, replica_groups=mesh['ens'=2,'dom'=8,'lat'=2] {'lat'}, dimensions={1} | all-to-all | bytes 327680 | tf_op jit(solution)/shard_map/all_to_all | solution.py:111
  153.7 4.9 %all_to_all.178 = bf16[1280,2,256]{0,2,1:T(8,128)(2,1)S(1)} all-to-all(bf16[1280,2,256]{0,2,1:T(8,128)(2,1)S(1)} %bitcast.66), channel_id=1, replica_groups=mesh['ens'=2,'dom'=8,'lat'=2] {'lat'}, dimensions={1} | all-to-all | bytes 2621440 | tf_op jit(solution)/shard_map/all_to_all | solution.py:110
  161.4 3.4 %fusion.4 = f32[1280,512]{1,0:T(8,128)} fusion(bf16[1280,512]{1,0:T(8,128)(2,1)S(1)} %copy-done.12, bf16[1536,512]{1,0:T(8,128)(2,1)} %param.24), kind=kOutput, calls=%fused_computation.23 | convolution fusion | flops 671744000 | bytes 4456448 | tf_op jit(solution)/shard_map/transpose(jvp())/dot_general | solution.py:26
  164.8 10.8 %scatter_fusion = f32[160,512]{1,0:T(8,128)S(1)} fusion(f32[160,512]{1,0:T(8,128)S(1)} %fusion.19, s32[1280]{0:T(1024)S(1)} %compare_select_fusion.3, f32[1280,512]{1,0:T(8,128)} %fusion.4), kind=kCustom, calls=%fused_computation.5 | custom fusion | flops 655360 | bytes 7869440 | tf_op jit(solution)/shard_map/transpose(jvp(jit(_take)))/scatter-add | solution.py:19
  178.3 5.8 %all_to_all.179 = f32[1280,2,256]{0,2,1:T(8,128)S(1)} all-to-all(f32[1280,2,256]{0,2,1:T(8,128)S(1)} %bitcast.68), channel_id=1, replica_groups=mesh['ens'=2,'dom'=8,'lat'=2] {'lat'}, dimensions={1} | all-to-all | bytes 5242880 | tf_op jit(solution)/shard_map/all_to_all | solution.py:115
  184.2 3.5 %all-to-all-start.7 = ((f32[160,2,256]{2,0,1:T(8,128)}), f32[160,2,256]{2,0,1:T(8,128)S(1)}, u32[]{:S(2)}, u32[]{:S(2)}) async-start(f32[160,2,256]{2,0,1:T(8,128)} %bitcast.59), calls=%async_computation.7 | async-start | bytes 655360 | tf_op jit(solution)/shard_map/all_to_all | solution.py:116
  189.7 22.7 %reduce-scatter.2.cloned.1.call-done = bf16[320,256]{1,0:T(8,128)(2,1)} async-done(((bf16[2560,256]{1,0:T(8,128)(2,1)}), bf16[320,256]{1,0:T(8,128)(2,1)}) %reduce-scatter.2.cloned.1.call-update) | async-done | bytes 163856 | tf_op jit(solution)/shard_map/reduce_scatter | solution.py:121
  (125 shorter events, 48.1 us)
Async XLA Ops:
  7.2 76.5 %copy-start = (bf16[512,512]{1,0:T(8,128)(2,1)S(1)}, bf16[512,512]{1,0:T(8,128)(2,1)}, u32[]{:S(2)}) copy-start(bf16[512,512]{1,0:T(8,128)(2,1)} %param.26) | copy-start | bytes 1572868
  7.2 9.3 %copy-start.18 = (bf16[2560,256]{1,0:T(8,128)(2,1)S(1)}, bf16[2560,256]{1,0:T(8,128)(2,1)}, u32[]{:S(2)}) copy-start(bf16[2560,256]{1,0:T(8,128)(2,1)} %param.20) | copy-start | bytes 3932164
  7.2 5.0 %all-to-all-start.5 = ((bf16[2,160,256]{2,1,0:T(8,128)(2,1)}), bf16[2,160,256]{2,1,0:T(8,128)(2,1)S(1)}, u32[]{:S(2)}, u32[]{:S(2)}) async-start(bf16[2,160,256]{2,1,0:T(8,128)(2,1)} %bitcast.86), calls=%async_computation.5 | async-start | bytes 327680 | tf_op jit(solution)/shard_map/all_to_all | solution.py:92
  10.8 44.6 %all-gather.2.cloned.1.call-start = ((), (), s32[]{:S(2)}) async-start(), calls=%async_computation.11 | async-start | bytes 1474560 | tf_op jit(solution)/shard_map/all_gather | solution.py:80
  12.2 5.7 %all-to-all-start = ((bf16[2,160,256]{2,1,0:T(8,128)(2,1)}), bf16[2,160,256]{2,1,0:T(8,128)(2,1)S(1)}, u32[]{:S(2)}, u32[]{:S(2)}) async-start(bf16[2,160,256]{2,1,0:T(8,128)(2,1)} %bitcast.82), calls=%async_computation | async-start | bytes 327680 | tf_op jit(solution)/shard_map/all_to_all | solution.py:91
  16.5 5.1 %copy-start.22 = (s32[2560]{0:T(1024)S(1)}, s32[2560]{0:T(1024)}, u32[]{:S(2)}) copy-start(s32[2560]{0:T(1024)} %param.22) | copy-start | bytes 30724
  16.5 5.2 %copy-start.2 = (s32[8,8,80]{2,1,0:T(8,128)S(1)}, s32[8,8,80]{2,1,0:T(8,128)}, u32[]{:S(2)}) copy-start(s32[8,8,80]{2,1,0:T(8,128)} %param.21) | copy-start | bytes 61444
  17.9 25.6 %all-to-all-start.1 = ((bf16[2,1280,256]{1,2,0:T(8,128)(2,1)}), bf16[2,1280,256]{1,2,0:T(8,128)(2,1)S(1)}, u32[]{:S(2)}, u32[]{:S(2)}) async-start(bf16[2,1280,256]{1,2,0:T(8,128)(2,1)} %copy.46), calls=%async_computation.1 | async-start | bytes 2621440 | tf_op jit(solution)/shard_map/all_to_all | solution.py:88
  21.6 14.5 %copy-start.19 = (bf16[2560,256]{1,0:T(8,128)(2,1)S(1)}, bf16[2560,256]{1,0:T(8,128)(2,1)}, u32[]{:S(2)}) copy-start(bf16[2560,256]{1,0:T(8,128)(2,1)} %param.37) | copy-start | bytes 3932164
  37.7 4.8 %copy-start.16 = (bf16[1024,512]{1,0:T(8,128)(2,1)S(1)}, bf16[1024,512]{1,0:T(8,128)(2,1)}, u32[]{:S(2)}) copy-start(bf16[1024,512]{1,0:T(8,128)(2,1)} %param.30) | copy-start | bytes 3145732
  73.1 40.6 %all-to-all-start.6 = ((bf16[2,1280,256]{1,2,0:T(8,128)(2,1)}), bf16[2,1280,256]{1,2,0:T(8,128)(2,1)}, u32[]{:S(2)}, u32[]{:S(2)}) async-start(bf16[2,1280,256]{1,2,0:T(8,128)(2,1)} %copy.52), calls=%async_computation.6 | async-start | bytes 2621440 | tf_op jit(solution)/shard_map/all_to_all | solution.py:90
  77.6 134.8 %reduce-scatter.2.cloned.1.call-start = ((), (), s32[]{:S(2)}) async-start(), calls=%async_computation.12 | async-start | bytes 1474560 | tf_op jit(solution)/shard_map/reduce_scatter | solution.py:121
  87.8 13.8 %copy-start.28 = (f32[512]{0:T(512)S(1)}, f32[512]{0:T(512)}, u32[]{:S(2)}) copy-start(f32[512]{0:T(512)} %param.31) | copy-start | bytes 6148
  87.8 15.4 %copy-start.32 = (f32[512]{0:T(512)S(1)}, f32[512]{0:T(512)}, u32[]{:S(2)}) copy-start(f32[512]{0:T(512)} %param.33) | copy-start | bytes 6148
  90.6 14.0 %copy-start.24 = (f32[512]{0:T(512)S(1)}, f32[512]{0:T(512)}, u32[]{:S(2)}) copy-start(f32[512]{0:T(512)} %param.34) | copy-start | bytes 6148
  90.6 14.3 %copy-start.29 = (f32[512]{0:T(512)S(1)}, f32[512]{0:T(512)}, u32[]{:S(2)}) copy-start(f32[512]{0:T(512)} %param.35) | copy-start | bytes 6148
  120.3 7.1 %copy-start.11 = (bf16[1280,512]{1,0:T(8,128)(2,1)}, bf16[1280,512]{1,0:T(8,128)(2,1)S(1)}, u32[]{:S(2)}) copy-start(bf16[1280,512]{1,0:T(8,128)(2,1)S(1)} %fusion.6) | copy-start | bytes 3932164
  146.0 7.7 %copy-start.7 = (bf16[1280,512]{0,1:T(8,128)(2,1)S(1)}, bf16[1280,512]{0,1:T(8,128)(2,1)}, u32[]{:S(2)}) copy-start(bf16[1280,512]{0,1:T(8,128)(2,1)} %add_convert_fusion) | copy-start | bytes 3932164
  153.7 6.3 %copy-start.10 = (f32[2,20,8,256]{3,2,0,1:T(8,128)S(1)}, f32[2,20,8,256]{3,2,0,1:T(8,128)}, u32[]{:S(2)}) copy-start(f32[2,20,8,256]{3,2,0,1:T(8,128)} %copy.60) | copy-start | bytes 983044
  153.7 6.3 %copy-start.21 = (bf16[160,512]{1,0:T(8,128)(2,1)S(1)}, bf16[160,512]{1,0:T(8,128)(2,1)}, u32[]{:S(2)}) copy-start(bf16[160,512]{1,0:T(8,128)(2,1)} %copy-done.20) | copy-start | bytes 491524
  164.8 11.5 %copy-start.6 = (bf16[1280,512]{0,1:T(8,128)(2,1)S(1)}, bf16[1280,512]{0,1:T(8,128)(2,1)}, u32[]{:S(2)}) copy-start(bf16[1280,512]{0,1:T(8,128)(2,1)} %copy-done.5) | copy-start | bytes 3932164
  164.8 11.5 %copy-start.13 = (bf16[1280,512]{1,0:T(8,128)(2,1)S(1)}, bf16[1280,512]{1,0:T(8,128)(2,1)}, u32[]{:S(2)}) copy-start(bf16[1280,512]{1,0:T(8,128)(2,1)} %copy-done.11) | copy-start | bytes 3932164
  184.2 5.6 %all-to-all-start.7 = ((f32[160,2,256]{2,0,1:T(8,128)}), f32[160,2,256]{2,0,1:T(8,128)S(1)}, u32[]{:S(2)}, u32[]{:S(2)}) async-start(f32[160,2,256]{2,0,1:T(8,128)} %bitcast.59), calls=%async_computation.7 | async-start | bytes 655360 | tf_op jit(solution)/shard_map/all_to_all | solution.py:116
  187.6 28.1 %copy-start.1 = (bf16[512,512]{1,0:T(8,128)(2,1)S(1)}, bf16[512,512]{1,0:T(8,128)(2,1)}, u32[]{:S(2)}) copy-start(bf16[512,512]{1,0:T(8,128)(2,1)} %param.26) | copy-start | bytes 1572868
  (16 other events, 34.6 us)
Sparse Core Ops, SparseCore 0:
  13.8 41.5 all-gather.1
  149.2 63.1 reduce-scatter.1
where the time goes:
time: 227 us; the launch traced here: 223 us
  local copies, waits for them, and re-layouts  57.2 us (25%)
  other arithmetic  50.5 us (22%)
  waiting for transfers between devices  32.7 us (14%)
  blocking collectives  25.7 us (11%)
  matrix products  23.2 us (10%)
  starting transfers between devices  18.7 us (8%)
  between operations  14.6 us (6%)
    reduce_scatter x1, waiting for transfers between devices, on_device(): lax.psum_scatter(spread.astype(jnp.bfloat16), 'dom', scatter_dimension=0,...  22.7 us
    scatter-add x1, other arithmetic, on_device(): jax.ops.segment_sum(sender_sums, global_row, num_segments=domains * node_...  16.3 us
    gather x1, local copies, waits for them, and re-layouts, on_device(): remote = halo_rows[source, member, offset % slot_count]  14.4 us
    scatter-add x1, other arithmetic, process(): jax.ops.segment_sum(edge_new.astype(jnp.float32), receiver, num_segments=...  11 us
    scatter-add x1, other arithmetic, process(): receiver_bf = jnp.take(node_full, receiver, axis=0).astype(jnp.bfloat16)  10.8 us
    gather x2, local copies, waits for them, and re-layouts, on_device(): sender_rows = jnp.take(everyone, global_row, axis=0)  10.7 us
    all_gather x1, waiting for transfers between devices, on_device(): everyone = lax.all_gather(node_lat, 'dom', axis=0, tiled=True)  8.48 us
    unnamed x67, local copies, waits for them, and re-layouts  7.34 us
  transfers between devices with their start and end apart: 7, of which 3 were waited for; matrix products, arithmetic and copies ran while one was open for 36% of the time, Pallas kernels for 0%

commit v1 on v0

v1 whole, which is shorter than its diff:
```python
import functools

import jax
import jax.numpy as jnp
from jax import lax
from jax.experimental import pallas as pl
from jax.experimental.pallas import tpu as pltpu
from jax.sharding import PartitionSpec as P

F32 = jnp.float32
BF16 = jnp.bfloat16


def mm(a, b):
    return jnp.dot(a, b, preferred_element_type=F32)


def mm_t(a, b):
    return lax.dot_general(a, b, (((1,), (1,)), ((), ())), preferred_element_type=F32)


def one_hot(match):
    return jnp.where(match, 1.0, 0.0).astype(BF16)


def column(row):
    return jnp.broadcast_to(row, (128, row.shape[1])).T


def across(col, depth):
    return one_hot(lax.broadcasted_iota(jnp.int32, (col.shape[0], depth), 1) == col[:, :1])


def down(row, height, first=0):
    return one_hot(lax.broadcasted_iota(jnp.int32, (height, row.shape[1]), 0) + first == row)


def activate(before):
    sig = 1.0 / (1.0 + jnp.exp(-before))
    return (before * sig).astype(BF16), sig * (1.0 + before * (1.0 - sig))


def normalise(output):
    centred = output - jnp.mean(output, axis=-1, keepdims=True)
    variance = jnp.mean(centred * centred, axis=-1, keepdims=True)
    rstd = lax.rsqrt(variance + 1e-05)
    return centred * rstd, rstd


def normalise_back(grad, xhat, rstd):
    first = jnp.mean(grad, axis=-1, keepdims=True)
    second = jnp.mean(grad * xhat, axis=-1, keepdims=True)
    return rstd * (grad - first - xhat * second)


def kernel(
    sizes,
    node_lat, edge_lat, node_ct, edge_ct,
    we_in, we_out, wn_in, wn_out,
    halo, sender, receiver,
    be_in, be_out, e_gain, e_shift, bn_in, bn_out, n_gain, n_shift,
    node_new, edge_new, edge_grad, node_grad,
    v_we_in, v_we_out, v_wn_in, v_wn_out, v_node,
    table, halo_buf, edges, edge_cts, node_cts,
    s_col, r_col, t_w, r_w, before, xhat_s, rstd_s, edge_s, node_s, dpre_s, grad_s,
    part, part_in, part_own, back_out, back_in, summed_s,
    w_sem, l_send, l_recv, r_send, r_recv, d_send, d_recv, b_send, b_recv,
):
    domains, rows, eb, nb, slots, width, tile, tiles = sizes
    p = lax.axis_index("dom")
    l = lax.axis_index("lat")
    o = 1 - l
    steps = eb // tile
    e_own = pl.ds(pl.multiple_of(l * eb, eb), eb)
    e_far = pl.ds(pl.multiple_of(o * eb, eb), eb)
    n_own = pl.ds(pl.multiple_of(l * nb, nb), nb)
    n_far = pl.ds(pl.multiple_of(o * nb, nb), nb)
    full = 2 * width

    barrier = pltpu.get_barrier_semaphore()

    def greet(d, c):
        pl.semaphore_signal(barrier, inc=1, device_id={"dom": lax.rem(p + d, domains)})
        return c

    lax.fori_loop(1, domains, greet, 0)
    pl.semaphore_signal(barrier, inc=1, device_id={"lat": o})

    local = [
        pltpu.make_async_copy(node_lat, v_node, w_sem.at[0]),
        pltpu.make_async_copy(we_in, v_we_in, w_sem.at[1]),
        pltpu.make_async_copy(node_lat, table.at[l, pl.ds(0, rows)], w_sem.at[2]),
        pltpu.make_async_copy(edge_lat.at[e_own], edges.at[l], w_sem.at[3]),
        pltpu.make_async_copy(we_out, v_we_out, w_sem.at[4]),
        pltpu.make_async_copy(wn_in, v_wn_in, w_sem.at[5]),
        pltpu.make_async_copy(wn_out, v_wn_out, w_sem.at[6]),
        pltpu.make_async_copy(node_ct.at[n_own], node_cts.at[l], w_sem.at[7]),
        pltpu.make_async_copy(edge_ct.at[e_own], edge_cts.at[l], w_sem.at[8]),
    ]
    for copy in local:
        copy.start()

    mine = pl.ds(pl.multiple_of(rows + p * slots, 16), slots)
    table[0, mine] = jnp.zeros((slots, width), BF16)
    table[1, mine] = jnp.zeros((slots, width), BF16)
    mine_back = pl.ds(pl.multiple_of(p * slots, 16), slots)
    back_in[mine_back] = jnp.zeros((slots, width), BF16)

    local[0].wait()
    for j in range(domains * slots // 128):
        col = column(halo[:, j * 128 : (j + 1) * 128])
        halo_buf[j * 128 : (j + 1) * 128] = mm(across(col, rows), v_node[...]).astype(BF16)

    pl.semaphore_wait(barrier, domains)

    def chunk(q):
        return pl.ds(pl.multiple_of(q * slots, 16), slots)

    def table_chunk(q):
        return pl.ds(pl.multiple_of(rows + q * slots, 16), slots)

    def dom_copy(q, source):
        return pltpu.make_async_remote_copy(
            src_ref=halo_buf.at[chunk(q)],
            dst_ref=table.at[l, table_chunk(source)],
            send_sem=d_send.at[q],
            recv_sem=d_recv.at[source],
            device_id={"dom": q},
        )

    def dom_start(d, c):
        dom_copy(lax.rem(p + d, domains), p).start()
        return c

    lax.fori_loop(1, domains, dom_start, 0)

    def lat_copy(src, dst, k):
        return pltpu.make_async_remote_copy(
            src_ref=src, dst_ref=dst, send_sem=l_send.at[k], recv_sem=l_recv.at[k], device_id={"lat": o}
        )

    to_lat = [
        lat_copy(node_lat, table.at[l, pl.ds(0, rows)], 0),
        lat_copy(edge_lat.at[e_far], edges.at[l], 1),
        lat_copy(node_ct.at[n_far], node_cts.at[l], 2),
        lat_copy(edge_ct.at[e_far], edge_cts.at[l], 3),
    ]
    for copy in to_lat:
        copy.start()

    def columns(i, c):
        at = pl.ds(pl.multiple_of(i * tile, tile), tile)
        lanes = pl.ds(pl.multiple_of(l * eb + i * tile, 128), tile)
        s_col[at] = column(sender[:, lanes])
        r_col[at] = column(receiver[:, lanes] - l * nb)
        return c

    lax.fori_loop(0, steps, columns, 0)

    local[1].wait()
    local[2].wait()
    to_lat[0].wait_recv()

    def both(ref, at):
        return jnp.concatenate([ref[0, at], ref[1, at]], axis=1)

    def halves(ref, at, value):
        ref[0, at] = value[:, :width]
        ref[1, at] = value[:, width:]

    w_e = v_we_in.at[pl.ds(0, full)]
    w_s = v_we_in.at[pl.ds(full, full)]
    w_r = v_we_in.at[pl.ds(2 * full, full)]
    wn_n = v_wn_in.at[pl.ds(0, full)]
    wn_s = v_wn_in.at[pl.ds(full, full)]

    node_full = both(table, n_own)
    r_w[...] = mm(node_full, w_r[...]).astype(BF16)

    def send_table(t, c):
        at = pl.ds(pl.multiple_of(t * rows, rows), rows)
        t_w[at] = mm(both(table, at), w_s[...]).astype(BF16)
        return c

    send_table(0, 0)
    if t_w.shape[0] > tiles * rows:
        t_w[tiles * rows :] = jnp.zeros((t_w.shape[0] - tiles * rows, full), BF16)

    local[3].wait()
    to_lat[1].wait_recv()

    def phase_a(i, c):
        at = pl.ds(pl.multiple_of(i * tile, tile), tile)
        value = mm(both(edges, at), w_e[...]) + mm(across(r_col[at], nb), r_w[...])
        before[at] = value + be_in[...]
        return c

    lax.fori_loop(0, steps, phase_a, 0)

    def relay_copy(q):
        return pltpu.make_async_remote_copy(
            src_ref=table.at[l, table_chunk(q)],
            dst_ref=table.at[l, table_chunk(q)],
            send_sem=r_send.at[q],
            recv_sem=r_recv.at[q],
            device_id={"lat": o},
        )

    def relay(d, c):
        q = lax.rem(p + domains - d, domains)
        dom_copy(q, q).wait_recv()
        relay_copy(q).start()
        return c

    lax.fori_loop(1, domains, relay, 0)

    def relayed(d, c):
        q = lax.rem(p + domains - d, domains)
        pltpu.make_async_remote_copy(
            src_ref=table.at[o, table_chunk(q)],
            dst_ref=table.at[o, table_chunk(q)],
            send_sem=r_send.at[q],
            recv_sem=r_recv.at[q],
            device_id={"lat": o},
        ).wait_recv()
        return c

    lax.fori_loop(1, domains, relayed, 0)
    lax.fori_loop(1, tiles, send_table, 0)
    local[4].wait()

    summed_s[...] = jnp.zeros_like(summed_s)

    def r_row(i):
        return receiver[:, pl.ds(pl.multiple_of(l * eb + i * tile, 128), tile)] - l * nb

    def phase_b(i, c):
        at = pl.ds(pl.multiple_of(i * tile, tile), tile)
        value = before[at] + mm(across(s_col[at], t_w.shape[0]), t_w[...])
        active, slope = activate(value)
        before[at] = slope
        xhat, rstd = normalise(mm(active, v_we_out[...]) + be_out[...])
        xhat_s[at] = xhat
        rstd_s[at] = jnp.broadcast_to(rstd, (tile, 128))
        fresh = (both(edges, at).astype(F32) + xhat * e_gain[...] + e_shift[...]).astype(BF16)
        halves(edge_s, at, fresh)
        summed_s[...] += mm(down(r_row(i), nb), fresh)
        return c

    lax.fori_loop(0, steps, phase_b, 0)

    edge_out = [
        pltpu.make_async_copy(edge_s.at[l], edge_new.at[e_own], w_sem.at[9]),
        lat_copy(edge_s.at[o], edge_new.at[e_own], 4),
    ]
    for copy in edge_out:
        copy.start()

    local[5].wait()
    local[6].wait()
    local[7].wait()
    to_lat[2].wait_recv()
    all_n = pl.ds(0, nb)
    node_full = both(table, n_own)
    active, slope = activate(
        mm(node_full, wn_n[...]) + mm(summed_s[...].astype(BF16), wn_s[...]) + bn_in[...]
    )
    xhat, rstd = normalise(mm(active, v_wn_out[...]) + bn_out[...])
    halves(
        node_s, all_n, (node_full.astype(F32) + xhat * n_gain[...] + n_shift[...]).astype(BF16)
    )
    node_out = [
        pltpu.make_async_copy(node_s.at[l], node_new.at[n_own], w_sem.at[10]),
        lat_copy(node_s.at[o], node_new.at[n_own], 5),
    ]
    for copy in node_out:
        copy.start()
    cot = both(node_cts, all_n).astype(F32)
    d_out = normalise_back(cot * n_gain[...], xhat, rstd).astype(BF16)
    d_before = (mm_t(d_out, v_wn_out[...]).astype(BF16).astype(F32) * slope).astype(BF16)
    node_part = cot + mm_t(d_before, wn_n[...]).astype(BF16).astype(F32)
    summed_s[...] = node_part
    r_w[...] = mm_t(d_before, wn_s[...]).astype(BF16)

    local[8].wait()
    to_lat[3].wait_recv()

    def phase_c(i, c):
        at = pl.ds(pl.multiple_of(i * tile, tile), tile)
        gathered = mm(across(r_col[at], nb), r_w[...])
        g = (both(edge_cts, at).astype(F32) + gathered).astype(BF16).astype(F32)
        rstd = rstd_s[at][:, :1]
        d_out = normalise_back(g * e_gain[...], xhat_s[at], rstd).astype(BF16)
        d_before = (mm_t(d_out, v_we_out[...]).astype(BF16).astype(F32) * before[at]).astype(BF16)
        dpre_s[at] = d_before
        halves(grad_s, at, (g + mm_t(d_before, w_e[...])).astype(BF16))
        return c

    lax.fori_loop(0, steps, phase_c, 0)

    row_lanes = pl.ds(pl.multiple_of(l * eb, 128), eb)

    def slot_part(t):
        hot = down(sender[:, row_lanes], rows, t * rows)
        return mm_t(mm(hot, dpre_s[...]).astype(BF16), w_s[...])

    def part_copy(t):
        at = pl.ds(pl.multiple_of(t * rows, rows), rows)
        return lat_copy(part.at[o, at], part_in.at[at], 7 + t)

    def parts(t, c):
        at = pl.ds(pl.multiple_of(t * rows, rows), rows)
        halves(part, at, slot_part(t).astype(BF16))
        part_copy(t).start()
        return c

    lax.fori_loop(1, tiles, parts, 0)

    def back_copy(q, source):
        return pltpu.make_async_remote_copy(
            src_ref=back_out.at[chunk(q)],
            dst_ref=back_in.at[chunk(source)],
            send_sem=b_send.at[q],
            recv_sem=b_recv.at[source],
            device_id={"dom": q},
        )

    per = rows // slots

    def back(t, c):
        at = pl.ds(pl.multiple_of(t * rows, rows), rows)
        part_copy(t).wait_recv()
        out = pl.ds(pl.multiple_of((t - 1) * rows, rows), rows)
        back_out[out] = (part[l, at].astype(F32) + part_in[at].astype(F32)).astype(BF16)
        for k in range(per):
            q = (t - 1) * per + k

            @pl.when(q != p)
            def _():
                back_copy(q, p).start()

        return c

    lax.fori_loop(1, tiles, back, 0)

    first = pl.ds(0, rows)
    halves(part_own, first, slot_part(0))
    hot = down(receiver[:, row_lanes] - l * nb, nb)
    node_part = summed_s[...] + mm_t(mm(hot, dpre_s[...]).astype(BF16), w_r[...])
    part_own[0, n_own] += node_part[:, :width]
    part_own[1, n_own] += node_part[:, width:]
    part[o, first] = part_own[o].astype(BF16)
    part_copy(0).start()

    grad_out = [
        pltpu.make_async_copy(grad_s.at[l], edge_grad.at[e_own], w_sem.at[11]),
        lat_copy(grad_s.at[o], edge_grad.at[e_own], 6),
    ]
    for copy in grad_out:
        copy.start()

    part_copy(0).wait_recv()

    def arrived(d, c):
        q = lax.rem(p + domains - d, domains)
        back_copy(q, q).wait_recv()
        return c

    lax.fori_loop(1, domains, arrived, 0)
    node_grad[...] = (
        part_own[l] + part_in[first].astype(F32) + mm(down(halo[...], rows), back_in[...])
    )

    def sent(d, c):
        q = lax.rem(p + d, domains)
        dom_copy(q, p).wait_send()
        relay_copy(q).wait_send()
        back_copy(q, p).wait_send()
        return c

    lax.fori_loop(1, domains, sent, 0)

    def parts_sent(t, c):
        part_copy(t).wait_send()
        return c

    lax.fori_loop(0, tiles, parts_sent, 0)
    for copy in to_lat:
        copy.wait_send()
    for pair in (edge_out, node_out, grad_out):
        pair[0].wait()
        pair[1].wait()


def on_device(
    node_lat, edge_lat, halo_rows, edge_sender, edge_receiver,
    edge_w_in, edge_b_in, edge_w_out, edge_b_out, edge_gain, edge_shift,
    node_w_in, node_b_in, node_w_out, node_b_out, node_gain, node_shift,
    node_ct, edge_ct,
):
    domains = lax.axis_size("dom")
    rows, width = node_lat.shape
    edge_rows = edge_lat.shape[0]
    slots = halo_rows.shape[2]
    eb, nb = edge_rows // 2, rows // 2
    full = 2 * width
    units = edge_w_out.shape[0]
    tile = 256
    tiles = 1 + domains * slots // rows
    slot_rows = tiles * rows
    depth = -(-slot_rows // 256) * 256
    halo = lax.dynamic_index_in_dim(halo_rows, lax.axis_index("dom"), 0, keepdims=False)
    halo = halo.reshape(1, domains * slots)
    any_spec = pl.BlockSpec(memory_space=pl.ANY)
    vmem = pl.BlockSpec(memory_space=pltpu.VMEM)
    dma = pltpu.SemaphoreType.DMA
    scratch = [
        pltpu.VMEM(edge_w_in.shape, BF16),
        pltpu.VMEM(edge_w_out.shape, BF16),
        pltpu.VMEM(node_w_in.shape, BF16),
        pltpu.VMEM(node_w_out.shape, BF16),
        pltpu.VMEM((rows, width), BF16),
        pltpu.VMEM((2, slot_rows, width), BF16),
        pltpu.VMEM((domains * slots, width), BF16),
        pltpu.VMEM((2, eb, width), BF16),
        pltpu.VMEM((2, eb, width), BF16),
        pltpu.VMEM((2, nb, width), BF16),
        pltpu.VMEM((eb, 128), jnp.int32),
        pltpu.VMEM((eb, 128), jnp.int32),
        pltpu.VMEM((depth, units), BF16),
        pltpu.VMEM((nb, units), BF16),
        pltpu.VMEM((eb, units), F32),
        pltpu.VMEM((eb, full), F32),
        pltpu.VMEM((eb, 128), F32),
        pltpu.VMEM((2, eb, width), BF16),
        pltpu.VMEM((2, nb, width), BF16),
        pltpu.VMEM((eb, units), BF16),
        pltpu.VMEM((2, eb, width), BF16),
        pltpu.VMEM((2, slot_rows, width), BF16),
        pltpu.VMEM((slot_rows, width), BF16),
        pltpu.VMEM((2, rows, width), F32),
        pltpu.VMEM((domains * slots, width), BF16),
        pltpu.VMEM((domains * slots, width), BF16),
        pltpu.VMEM((nb, full), F32),
        dma((12,)),
        dma((7 + tiles,)),
        dma((7 + tiles,)),
    ] + [dma((domains,)) for _ in range(6)]
    sizes = (domains, rows, eb, nb, slots, width, tile, tiles)

    def line(x):
        return x.reshape(1, -1)

    node_new, edge_new, edge_grad, node_grad = pl.pallas_call(
        functools.partial(kernel, sizes),
        out_shape=(
            jax.ShapeDtypeStruct((rows, width), BF16),
            jax.ShapeDtypeStruct((edge_rows, width), BF16),
            jax.ShapeDtypeStruct((edge_rows, width), BF16),
            jax.ShapeDtypeStruct((rows, width), F32),
        ),
        in_specs=[any_spec] * 8 + [vmem] * 11,
        out_specs=(any_spec, any_spec, any_spec, vmem),
        scratch_shapes=scratch,
        compiler_params=pltpu.CompilerParams(
            collective_id=0, has_side_effects=True, vmem_limit_bytes=48 * 1024 * 1024
        ),
    )(
        node_lat, edge_lat, node_ct, edge_ct,
        edge_w_in, edge_w_out, node_w_in, node_w_out,
        halo, line(edge_sender), line(edge_receiver),
        line(edge_b_in), line(edge_b_out), line(edge_gain), line(edge_shift),
        line(node_b_in), line(node_b_out), line(node_gain), line(node_shift),
    )
    return (node_new, edge_new, node_grad, edge_grad.astype(F32))


def solution(mesh):
    many = P(("ens", "dom"), "lat")
    return jax.shard_map(
        on_device,
        mesh=mesh,
        in_specs=(many, many, P("ens", None, None), P(("ens", "dom")), P(("ens", "dom")))
        + (P(),) * 12
        + (many, many),
        out_specs=(many,) * 4,
        check_vma=False,
    )
```

time: 227 us -> 56.5 us (0.25); the launches traced: 223 us -> 55.9 us
  other arithmetic: 50.5 us -> 1.69 us
  local copies, waits for them, and re-layouts: 57.2 us -> 15.3 us
  Pallas kernels: 0 us -> 38.2 us
  waiting for transfers between devices: 32.7 us -> 0 us
  blocking collectives: 25.7 us -> 0 us
  matrix products: 23.2 us -> 0 us
  starting transfers between devices: 18.7 us -> 0 us
  between operations: 14.6 us -> 0.67 us
    pallas_call x0 -> x1, Pallas kernels: none -> 38.2 us  [on_device(): pl.pallas_call(functools.partial(kernel, sizes), out_shape=(jax.ShapeDtyp...]
    scatter-add x3 -> x0, other arithmetic: 38 us -> none  [the longest x1 16.3 us: on_device(): jax.ops.segment_sum(sender_sums, global_row, num_segments=domains * node_...]
    gather x6 -> x0, local copies, waits for them, and re-layouts: 37 us -> none  [the longest x1 14.4 us: on_device(): remote = halo_rows[source, member, offset % slot_count]]
    all_to_all x5 -> x0, blocking collectives: 25.7 us -> none  [the longest x1 5.84 us: on_device(): lax.all_to_all(edge_grad, 'lat', split_axis=1, concat_axis=0, tiled=True)]
    dot_general x14 -> x0, matrix products: 23.2 us -> none  [the longest x2 5.37 us: process(): jnp.dot(receiver_bf, w_edge[2 * width:], preferred_element_type=jnp.float32)]
    reduce_scatter x1 -> x0, waiting for transfers between devices: 22.7 us -> none  [on_device(): lax.psum_scatter(spread.astype(jnp.bfloat16), 'dom', scatter_dimension=0,...]
    all_to_all x5 -> x0, starting transfers between devices: 18.6 us -> none  [the longest x1 4.5 us: on_device(): lax.all_to_all(edge_ct, 'lat', split_axis=0, concat_axis=1, tiled=True)]
    all_gather x1 -> x0, waiting for transfers between devices: 8.48 us -> none  [on_device(): everyone = lax.all_gather(node_lat, 'dom', axis=0, tiled=True)]
  transfers between devices with their start and end apart: 7 -> 0, of which waited for: 3 -> 0; matrix products, arithmetic and copies ran while one was open for 36% -> 0% of each run, Pallas kernels for 0% -> 0%
where the time goes in v1:
time: 56.5 us; the launch traced here: 55.9 us
  Pallas kernels  38.2 us (68%)
  local copies, waits for them, and re-layouts  15.3 us (27%)
  other arithmetic  1.69 us (3%)
  between operations  0.67 us (1%)
    pallas_call x1, Pallas kernels, on_device(): pl.pallas_call(functools.partial(kernel, sizes), out_shape=(jax.ShapeDtyp...  38.2 us
    unnamed x31, local copies, waits for them, and re-layouts  13.8 us
    convert_element_type x1, other arithmetic, on_device(): return (node_new, edge_new, node_grad, edge_grad.astype(F32))  1.69 us
    reshape x2, local copies, waits for them, and re-layouts, line(): return x.reshape(1, -1)  1.43 us

profile of v1, /device:TPU:26, one launch (start us, length us, event | category | flops | bytes accessed | tf_op | source)
XLA Modules:
  0.0 55.9 jit_solution(12851792882698623363)
XLA Ops:
  0.6 0.0 copy-start
  0.6 0.7 %copy-done = s32[8,8,80]{2,1,0:T(8,128)S(1)} copy-done((s32[8,8,80]{2,1,0:T(8,128)S(1)}, s32[8,8,80]{2,1,0:T(8,128)}, u32[]{:S(2)}) %copy-start) | copy-done | bytes 20504
  1.4 0.1 reshape.42.halo
  1.5 0.7 %reshape.43.sender = s32[1,2560]{1,0:T(1,128)S(1)} reshape(s32[2560]{0:T(1024)} %param.22) | data formatting | bytes 20480 | tf_op jit(solution)/shard_map/reshape | solution.py:452
  2.2 0.7 %reshape.44.receiver = s32[1,2560]{1,0:T(1,128)S(1)} reshape(s32[2560]{0:T(1024)} %param.23) | data formatting | bytes 20480 | tf_op jit(solution)/shard_map/reshape | solution.py:452
  2.9 1.2 %copy-done.1 = bf16[1024,512]{1,0:T(8,128)(2,1)S(1)} copy-done((bf16[1024,512]{1,0:T(8,128)(2,1)S(1)}, bf16[1024,512]{1,0:T(8,128)(2,1)}, u32[]{:S(2)}) %copy-start.1) | copy-done | bytes 1048600
  4.1 0.0 copy-start.2
  4.1 1.0 %copy-done.2 = bf16[512,512]{1,0:T(8,128)(2,1)S(1)} copy-done((bf16[512,512]{1,0:T(8,128)(2,1)S(1)}, bf16[512,512]{1,0:T(8,128)(2,1)}, u32[]{:S(2)}) %copy-start.2) | copy-done | bytes 524312
  5.2 1.0 %copy-done.3 = bf16[512,512]{1,0:T(8,128)(2,1)S(1)} copy-done((bf16[512,512]{1,0:T(8,128)(2,1)S(1)}, bf16[512,512]{1,0:T(8,128)(2,1)}, u32[]{:S(2)}) %copy-start.3) | copy-done | bytes 524312
  6.2 0.9 %copy-done.4 = bf16[320,256]{1,0:T(8,128)(2,1)S(1)} copy-done((bf16[320,256]{1,0:T(8,128)(2,1)S(1)}, bf16[320,256]{1,0:T(8,128)(2,1)}, u32[]{:S(2)}) %copy-start.4) | copy-done | bytes 163864
  7.1 0.9 %copy-done.5 = bf16[320,256]{1,0:T(8,128)(2,1)S(1)} copy-done((bf16[320,256]{1,0:T(8,128)(2,1)S(1)}, bf16[320,256]{1,0:T(8,128)(2,1)}, u32[]{:S(2)}) %copy-start.5) | copy-done | bytes 163864
  8.1 0.7 %copy-done.6 = f32[512]{0:T(512)S(1)} copy-done((f32[512]{0:T(512)S(1)}, f32[512]{0:T(512)}, u32[]{:S(2)}) %copy-start.6) | copy-done | bytes 2072
  8.7 0.7 %copy-done.7 = f32[512]{0:T(512)S(1)} copy-done((f32[512]{0:T(512)S(1)}, f32[512]{0:T(512)}, u32[]{:S(2)}) %copy-start.7) | copy-done | bytes 2072
  9.4 0.7 %copy-done.8 = f32[512]{0:T(512)S(1)} copy-done((f32[512]{0:T(512)S(1)}, f32[512]{0:T(512)}, u32[]{:S(2)}) %copy-start.8) | copy-done | bytes 2072
  10.1 0.7 %copy-done.9 = f32[512]{0:T(512)S(1)} copy-done((f32[512]{0:T(512)S(1)}, f32[512]{0:T(512)}, u32[]{:S(2)}) %copy-start.9) | copy-done | bytes 2072
  10.8 0.7 %copy-done.10 = f32[512]{0:T(512)S(1)} copy-done((f32[512]{0:T(512)S(1)}, f32[512]{0:T(512)}, u32[]{:S(2)}) %copy-start.10) | copy-done | bytes 2072
  11.5 0.7 %copy-done.11 = f32[512]{0:T(512)S(1)} copy-done((f32[512]{0:T(512)S(1)}, f32[512]{0:T(512)}, u32[]{:S(2)}) %copy-start.11) | copy-done | bytes 2072
  12.2 0.7 %copy-done.12 = f32[512]{0:T(512)S(1)} copy-done((f32[512]{0:T(512)S(1)}, f32[512]{0:T(512)}, u32[]{:S(2)}) %copy-start.12) | copy-done | bytes 2072
  12.8 0.7 %copy-done.13 = f32[512]{0:T(512)S(1)} copy-done((f32[512]{0:T(512)S(1)}, f32[512]{0:T(512)}, u32[]{:S(2)}) %copy-start.13) | copy-done | bytes 2072
  13.5 38.2 %shard_map.210 = (bf16[320,256]{1,0:T(8,128)(2,1)S(1)}, bf16[2560,256]{1,0:T(8,128)(2,1)S(1)}, bf16[2560,256]{1,0:T(8,128)(2,1)S(1)}, f32[320,256]{1,0:T(8,128)S(1)}) custom-call(bf16[320,256]{1,0:T(8,128)(2,1)S(1)} %copy-done.4, bf16[2560,256]{1,0:T(8,128)(2,1)} %edge_lat.1, bf16[320,256]{1,0:T(8,128)(2,1)S(1)} %copy-done.5, bf16[2560,256]{1,0:T(8,128)(2,1)} %edge_ct.1, ...), custom_call_target="tpu_custom_call" | custom-call | tf_op jit(solution)/shard_map/pallas_call | solution.py:454
  51.8 1.7 %convert_element_type.3 = f32[2560,256]{1,0:T(8,128)} convert(bf16[2560,256]{1,0:T(8,128)(2,1)S(1)} %get-tuple-element.11) | non-fusion elementwise | flops 655360 | bytes 3932160 | tf_op jit(solution)/shard_map/convert_element_type | solution.py:475
  53.4 0.7 %copy.26 = bf16[320,256]{1,0:T(8,128)(2,1)} copy(bf16[320,256]{1,0:T(8,128)(2,1)S(1)} %get-tuple-element.16) | data formatting | bytes 327680
  54.1 1.1 %copy.27 = bf16[2560,256]{1,0:T(8,128)(2,1)} copy(bf16[2560,256]{1,0:T(8,128)(2,1)S(1)} %get-tuple-element.17) | data formatting | bytes 2621440
  55.2 0.7 %copy.28 = f32[320,256]{1,0:T(8,128)} copy(f32[320,256]{1,0:T(8,128)S(1)} %get-tuple-element.18) | data formatting | bytes 655360
  (13 shorter events, 0.0 us)
Async XLA Ops:
  0.6 0.8 %copy-start = (s32[8,8,80]{2,1,0:T(8,128)S(1)}, s32[8,8,80]{2,1,0:T(8,128)}, u32[]{:S(2)}) copy-start(s32[8,8,80]{2,1,0:T(8,128)} %param.21) | copy-start | bytes 61444
  2.9 1.2 %copy-start.1 = (bf16[1024,512]{1,0:T(8,128)(2,1)S(1)}, bf16[1024,512]{1,0:T(8,128)(2,1)}, u32[]{:S(2)}) copy-start(bf16[1024,512]{1,0:T(8,128)(2,1)} %wn_in.1) | copy-start | bytes 3145732
  4.1 1.0 %copy-start.2 = (bf16[512,512]{1,0:T(8,128)(2,1)S(1)}, bf16[512,512]{1,0:T(8,128)(2,1)}, u32[]{:S(2)}) copy-start(bf16[512,512]{1,0:T(8,128)(2,1)} %we_out.1) | copy-start | bytes 1572868
  5.2 1.0 %copy-start.3 = (bf16[512,512]{1,0:T(8,128)(2,1)S(1)}, bf16[512,512]{1,0:T(8,128)(2,1)}, u32[]{:S(2)}) copy-start(bf16[512,512]{1,0:T(8,128)(2,1)} %wn_out.1) | copy-start | bytes 1572868
  6.2 0.9 %copy-start.4 = (bf16[320,256]{1,0:T(8,128)(2,1)S(1)}, bf16[320,256]{1,0:T(8,128)(2,1)}, u32[]{:S(2)}) copy-start(bf16[320,256]{1,0:T(8,128)(2,1)} %node_lat.1) | copy-start | bytes 491524
  7.1 0.9 %copy-start.5 = (bf16[320,256]{1,0:T(8,128)(2,1)S(1)}, bf16[320,256]{1,0:T(8,128)(2,1)}, u32[]{:S(2)}) copy-start(bf16[320,256]{1,0:T(8,128)(2,1)} %node_ct.1) | copy-start | bytes 491524
  8.1 0.7 %copy-start.6 = (f32[512]{0:T(512)S(1)}, f32[512]{0:T(512)}, u32[]{:S(2)}) copy-start(f32[512]{0:T(512)} %param.25) | copy-start | bytes 6148
  8.7 0.7 %copy-start.7 = (f32[512]{0:T(512)S(1)}, f32[512]{0:T(512)}, u32[]{:S(2)}) copy-start(f32[512]{0:T(512)} %param.27) | copy-start | bytes 6148
  9.4 0.7 %copy-start.8 = (f32[512]{0:T(512)S(1)}, f32[512]{0:T(512)}, u32[]{:S(2)}) copy-start(f32[512]{0:T(512)} %param.28) | copy-start | bytes 6148
  10.1 0.7 %copy-start.9 = (f32[512]{0:T(512)S(1)}, f32[512]{0:T(512)}, u32[]{:S(2)}) copy-start(f32[512]{0:T(512)} %param.29) | copy-start | bytes 6148
  10.8 0.7 %copy-start.10 = (f32[512]{0:T(512)S(1)}, f32[512]{0:T(512)}, u32[]{:S(2)}) copy-start(f32[512]{0:T(512)} %param.31) | copy-start | bytes 6148
  11.5 0.7 %copy-start.11 = (f32[512]{0:T(512)S(1)}, f32[512]{0:T(512)}, u32[]{:S(2)}) copy-start(f32[512]{0:T(512)} %param.33) | copy-start | bytes 6148
  12.1 0.7 %copy-start.12 = (f32[512]{0:T(512)S(1)}, f32[512]{0:T(512)}, u32[]{:S(2)}) copy-start(f32[512]{0:T(512)} %param.34) | copy-start | bytes 6148
  12.8 0.7 %copy-start.13 = (f32[512]{0:T(512)S(1)}, f32[512]{0:T(512)}, u32[]{:S(2)}) copy-start(f32[512]{0:T(512)} %param.35) | copy-start | bytes 6148

commit v2 on v1

--- a/solution.py
+++ b/solution.py
@@ -9,6 +9,7 @@
 
 F32 = jnp.float32
 BF16 = jnp.bfloat16
+UNROLL = True
 
 
 def mm(a, b):
@@ -36,7 +37,7 @@
 
 
 def activate(before):
-    sig = 1.0 / (1.0 + jnp.exp(-before))
+    sig = 0.5 + 0.5 * jnp.tanh(0.5 * before)
     return (before * sig).astype(BF16), sig * (1.0 + before * (1.0 - sig))
 
 
@@ -57,14 +58,16 @@
     sizes,
     node_lat, edge_lat, node_ct, edge_ct,
     we_in, we_out, wn_in, wn_out,
-    halo, sender, receiver,
+    halo_h, sender_h, receiver_h,
+    h0, h1, h2, h3, h4, h5, h6, h7,
+    node_new, edge_new, edge_grad, node_grad,
+    halo, sender_v, receiver_v, sender, receiver,
     be_in, be_out, e_gain, e_shift, bn_in, bn_out, n_gain, n_shift,
-    node_new, edge_new, edge_grad, node_grad,
     v_we_in, v_we_out, v_wn_in, v_wn_out, v_node,
     table, halo_buf, edges, edge_cts, node_cts,
-    s_col, r_col, t_w, r_w, before, xhat_s, rstd_s, edge_s, node_s, dpre_s, grad_s,
+    s_col, r_col, t_w, own_w, r_w, before, xhat_s, rstd_s, edge_s, node_s, dpre_s, grad_s,
     part, part_in, part_own, back_out, back_in, summed_s,
-    w_sem, l_send, l_recv, r_send, r_recv, d_send, d_recv, b_send, b_recv,
+    i_sem, w_sem, l_send, l_recv, r_send, r_recv, d_send, d_recv, b_send, b_recv,
 ):
     domains, rows, eb, nb, slots, width, tile, tiles = sizes
     p = lax.axis_index("dom")
@@ -77,6 +80,16 @@
     n_far = pl.ds(pl.multiple_of(o * nb, nb), nb)
     full = 2 * width
 
+    small = [
+        pltpu.make_async_copy(src, dst, i_sem.at[k])
+        for k, (src, dst) in enumerate(
+            (
+                (halo_h, halo), (sender_h, sender_v), (receiver_h, receiver_v),
+                (h0, be_in), (h1, be_out), (h2, e_gain), (h3, e_shift),
+                (h4, bn_in), (h5, bn_out), (h6, n_gain), (h7, n_shift),
+            )
+        )
+    ]
     barrier = pltpu.get_barrier_semaphore()
 
     def greet(d, c):
@@ -97,7 +110,9 @@
         pltpu.make_async_copy(node_ct.at[n_own], node_cts.at[l], w_sem.at[7]),
         pltpu.make_async_copy(edge_ct.at[e_own], edge_cts.at[l], w_sem.at[8]),
     ]
-    for copy in local:
+    small[0].start()
+    local[0].start()
+    for copy in small[1:] + local[1:]:
         copy.start()
 
     mine = pl.ds(pl.multiple_of(rows + p * slots, 16), slots)
@@ -106,6 +121,7 @@
     mine_back = pl.ds(pl.multiple_of(p * slots, 16), slots)
     back_in[mine_back] = jnp.zeros((slots, width), BF16)
 
+    small[0].wait()
     local[0].wait()
     for j in range(domains * slots // 128):
         col = column(halo[:, j * 128 : (j + 1) * 128])
@@ -148,14 +164,17 @@
     for copy in to_lat:
         copy.start()
 
-    def columns(i, c):
-        at = pl.ds(pl.multiple_of(i * tile, tile), tile)
-        lanes = pl.ds(pl.multiple_of(l * eb + i * tile, 128), tile)
-        s_col[at] = column(sender[:, lanes])
-        r_col[at] = column(receiver[:, lanes] - l * nb)
-        return c
-
-    lax.fori_loop(0, steps, columns, 0)
+    small[1].wait()
+    small[2].wait()
+    groups = eb // 128
+    for j in range(groups):
+        at = pl.ds(j * 128, 128)
+        sender[:, at] = sender_v[pl.ds(l * groups + j, 1), :]
+        receiver[:, at] = receiver_v[pl.ds(l * groups + j, 1), :] - l * nb
+        s_col[at] = column(sender[:, at])
+        r_col[at] = column(receiver[:, at])
+    for copy in small[3:]:
+        copy.wait()
 
     local[1].wait()
     local[2].wait()
@@ -175,27 +194,34 @@
     wn_s = v_wn_in.at[pl.ds(full, full)]
 
     node_full = both(table, n_own)
-    r_w[...] = mm(node_full, w_r[...]).astype(BF16)
+    near = own_w.shape[0]
+    own_w[rows : rows + nb] = mm(node_full, w_r[...]).astype(BF16)
+    own_w[:rows] = mm(both(table, pl.ds(0, rows)), w_s[...]).astype(BF16)
+    if near > rows + nb:
+        own_w[rows + nb :] = jnp.zeros((near - rows - nb, full), BF16)
 
     def send_table(t, c):
         at = pl.ds(pl.multiple_of(t * rows, rows), rows)
-        t_w[at] = mm(both(table, at), w_s[...]).astype(BF16)
-        return c
-
-    send_table(0, 0)
-    if t_w.shape[0] > tiles * rows:
-        t_w[tiles * rows :] = jnp.zeros((t_w.shape[0] - tiles * rows, full), BF16)
+        to = pl.ds(pl.multiple_of((t - 1) * rows, rows), rows)
+        t_w[to] = mm(both(table, at), w_s[...]).astype(BF16)
+        return c
+
+    if t_w.shape[0] > (tiles - 1) * rows:
+        t_w[(tiles - 1) * rows :] = jnp.zeros((t_w.shape[0] - (tiles - 1) * rows, full), BF16)
 
     local[3].wait()
     to_lat[1].wait_recv()
 
     def phase_a(i, c):
         at = pl.ds(pl.multiple_of(i * tile, tile), tile)
-        value = mm(both(edges, at), w_e[...]) + mm(across(r_col[at], nb), r_w[...])
+        lane = lax.broadcasted_iota(jnp.int32, (tile, near), 1)
+        from_own = jnp.where(s_col[at][:, :1] < rows, s_col[at][:, :1], -1)
+        hot = one_hot((lane == from_own) | (lane == r_col[at][:, :1] + rows))
+        value = mm(both(edges, at), w_e[...]) + mm(hot, own_w[...])
         before[at] = value + be_in[...]
         return c
 
-    lax.fori_loop(0, steps, phase_a, 0)
+    lax.fori_loop(0, steps, phase_a, 0, unroll=UNROLL)
 
     def relay_copy(q):
         return pltpu.make_async_remote_copy(
@@ -232,11 +258,11 @@
     summed_s[...] = jnp.zeros_like(summed_s)
 
     def r_row(i):
-        return receiver[:, pl.ds(pl.multiple_of(l * eb + i * tile, 128), tile)] - l * nb
+        return receiver[:, pl.ds(pl.multiple_of(i * tile, 128), tile)]
 
     def phase_b(i, c):
         at = pl.ds(pl.multiple_of(i * tile, tile), tile)
-        value = before[at] + mm(across(s_col[at], t_w.shape[0]), t_w[...])
+        value = before[at] + mm(across(s_col[at] - rows, t_w.shape[0]), t_w[...])
         active, slope = activate(value)
         before[at] = slope
         xhat, rstd = normalise(mm(active, v_we_out[...]) + be_out[...])
@@ -247,7 +273,7 @@
         summed_s[...] += mm(down(r_row(i), nb), fresh)
         return c
 
-    lax.fori_loop(0, steps, phase_b, 0)
+    lax.fori_loop(0, steps, phase_b, 0, unroll=UNROLL)
 
     edge_out = [
         pltpu.make_async_copy(edge_s.at[l], edge_new.at[e_own], w_sem.at[9]),
@@ -288,20 +314,19 @@
     def phase_c(i, c):
         at = pl.ds(pl.multiple_of(i * tile, tile), tile)
         gathered = mm(across(r_col[at], nb), r_w[...])
-        g = (both(edge_cts, at).astype(F32) + gathered).astype(BF16).astype(F32)
+        g = (both(edge_cts, at).astype(F32) + gathered).astype(BF16)
+        halves(edge_cts, at, g)
+        g = g.astype(F32)
         rstd = rstd_s[at][:, :1]
         d_out = normalise_back(g * e_gain[...], xhat_s[at], rstd).astype(BF16)
         d_before = (mm_t(d_out, v_we_out[...]).astype(BF16).astype(F32) * before[at]).astype(BF16)
         dpre_s[at] = d_before
-        halves(grad_s, at, (g + mm_t(d_before, w_e[...])).astype(BF16))
-        return c
-
-    lax.fori_loop(0, steps, phase_c, 0)
-
-    row_lanes = pl.ds(pl.multiple_of(l * eb, 128), eb)
+        return c
+
+    lax.fori_loop(0, steps, phase_c, 0, unroll=UNROLL)
 
     def slot_part(t):
-        hot = down(sender[:, row_lanes], rows, t * rows)
+        hot = down(sender[...], rows, t * rows)
         return mm_t(mm(hot, dpre_s[...]).astype(BF16), w_s[...])
 
     def part_copy(t):
@@ -345,12 +370,20 @@
 
     first = pl.ds(0, rows)
     halves(part_own, first, slot_part(0))
-    hot = down(receiver[:, row_lanes] - l * nb, nb)
+    hot = down(receiver[...], nb)
     node_part = summed_s[...] + mm_t(mm(hot, dpre_s[...]).astype(BF16), w_r[...])
     part_own[0, n_own] += node_part[:, :width]
     part_own[1, n_own] += node_part[:, width:]
     part[o, first] = part_own[o].astype(BF16)
     part_copy(0).start()
+
+    def phase_d(i, c):
+        at = pl.ds(pl.multiple_of(i * tile, tile), tile)
+        g = both(edge_cts, at).astype(F32)
+        halves(grad_s, at, (g + mm_t(dpre_s[at], w_e[...])).astype(BF16))
+        return c
+
+    lax.fori_loop(0, steps, phase_d, 0, unroll=UNROLL)
 
     grad_out = [
         pltpu.make_async_copy(grad_s.at[l], edge_grad.at[e_own], w_sem.at[11]),
@@ -408,13 +441,20 @@
     tile = 256
     tiles = 1 + domains * slots // rows
     slot_rows = tiles * rows
-    depth = -(-slot_rows // 256) * 256
+    depth = -(-(slot_rows - rows) // 128) * 128
+    near = -(-(rows + nb) // 256) * 256
     halo = lax.dynamic_index_in_dim(halo_rows, lax.axis_index("dom"), 0, keepdims=False)
     halo = halo.reshape(1, domains * slots)
     any_spec = pl.BlockSpec(memory_space=pl.ANY)
     vmem = pl.BlockSpec(memory_space=pltpu.VMEM)
     dma = pltpu.SemaphoreType.DMA
     scratch = [
+        pltpu.VMEM((1, domains * slots), jnp.int32),
+        pltpu.VMEM((edge_rows // 128, 128), jnp.int32),
+        pltpu.VMEM((edge_rows // 128, 128), jnp.int32),
+        pltpu.VMEM((1, eb), jnp.int32),
+        pltpu.VMEM((1, eb), jnp.int32),
+    ] + [pltpu.VMEM((1, full), F32) for _ in range(8)] + [
         pltpu.VMEM(edge_w_in.shape, BF16),
         pltpu.VMEM(edge_w_out.shape, BF16),
         pltpu.VMEM(node_w_in.shape, BF16),
@@ -428,6 +468,7 @@
         pltpu.VMEM((eb, 128), jnp.int32),
         pltpu.VMEM((eb, 128), jnp.int32),
         pltpu.VMEM((depth, units), BF16),
+        pltpu.VMEM((near, units), BF16),
         pltpu.VMEM((nb, units), BF16),
         pltpu.VMEM((eb, units), F32),
         pltpu.VMEM((eb, full), F32),
@@ -442,6 +483,7 @@
         pltpu.VMEM((domains * slots, width), BF16),
         pltpu.VMEM((domains * slots, width), BF16),
         pltpu.VMEM((nb, full), F32),
+        dma((11,)),
         dma((12,)),
         dma((7 + tiles,)),
         dma((7 + tiles,)),
@@ -459,16 +501,16 @@
             jax.ShapeDtypeStruct((edge_rows, width), BF16),
             jax.ShapeDtypeStruct((rows, width), F32),
         ),
-        in_specs=[any_spec] * 8 + [vmem] * 11,
+        in_specs=[any_spec] * 19,
         out_specs=(any_spec, any_spec, any_spec, vmem),
         scratch_shapes=scratch,
         compiler_params=pltpu.CompilerParams(
-            collective_id=0, has_side_effects=True, vmem_limit_bytes=48 * 1024 * 1024
+            collective_id=0, has_side_effects=True, vmem_limit_bytes=60 * 1024 * 1024
         ),
     )(
         node_lat, edge_lat, node_ct, edge_ct,
         edge_w_in, edge_w_out, node_w_in, node_w_out,
-        halo, line(edge_sender), line(edge_receiver),
+        halo, edge_sender.reshape(-1, 128), edge_receiver.reshape(-1, 128),
         line(edge_b_in), line(edge_b_out), line(edge_gain), line(edge_shift),
         line(node_b_in), line(node_b_out), line(node_gain), line(node_shift),
     )

time: 56.5 us -> 43.7 us (0.77)
  local copies, waits for them, and re-layouts: 15.3 us -> 3.98 us
  Pallas kernels: 38.2 us -> 35.6 us
  other arithmetic: 1.69 us -> 3.12 us
    unnamed x31 -> x11, local copies, waits for them, and re-layouts: 13.8 us -> 3.31 us
    pallas_call x1, Pallas kernels: 38.2 us -> 35.6 us  [on_device(): pl.pallas_call(functools.partial(kernel, sizes), out_shape=(jax.ShapeDtyp...]
    reshape x2 -> x0, local copies, waits for them, and re-layouts: 1.43 us -> none  [line(): return x.reshape(1, -1)]
    convert_element_type x1, other arithmetic: 1.69 us -> 3.12 us  [on_device(): return (node_new, edge_new, node_grad, edge_grad.astype(F32))]
    reshape x1, local copies, waits for them, and re-layouts: 0.08 us -> 0.66 us  [on_device(): halo = halo.reshape(1, domains * slots)]
where the time goes in v2:
time: 43.7 us; the launch traced here: 43.4 us
  Pallas kernels  35.6 us (81%)
  local copies, waits for them, and re-layouts  3.98 us (9%)
  other arithmetic  3.12 us (7%)
  between operations  0.67 us (2%)
    pallas_call x1, Pallas kernels, on_device(): pl.pallas_call(functools.partial(kernel, sizes), out_shape=(jax.ShapeDtyp...  35.6 us
    unnamed x11, local copies, waits for them, and re-layouts  3.31 us
    convert_element_type x1, other arithmetic, on_device(): return (node_new, edge_new, node_grad, edge_grad.astype(F32))  3.12 us

profile of v2, /device:TPU:26, one launch (start us, length us, event | category | flops | bytes accessed | tf_op | source)
XLA Modules:
  0.0 43.4 jit_solution(6687932025610046030)
XLA Ops:
  0.6 0.0 copy-start
  0.6 0.7 %copy-done = s32[8,8,80]{2,1,0:T(8,128)S(1)} copy-done((s32[8,8,80]{2,1,0:T(8,128)S(1)}, s32[8,8,80]{2,1,0:T(8,128)}, u32[]{:S(2)}) %copy-start) | copy-done | bytes 20504
  1.4 0.7 %reshape.42.halo_h = s32[1,640]{1,0:T(1,128)} reshape(s32[1,8,80]{2,1,0:T(8,128)S(1)} %constant_dynamic-slice_fusion) | data formatting | bytes 5120 | tf_op jit(solution)/shard_map/reshape | solution.py:447
  2.1 35.6 %shard_map.210 = (bf16[320,256]{1,0:T(8,128)(2,1)}, bf16[2560,256]{1,0:T(8,128)(2,1)}, bf16[2560,256]{1,0:T(8,128)(2,1)}, f32[320,256]{1,0:T(8,128)}) custom-call(bf16[320,256]{1,0:T(8,128)(2,1)} %node_lat.1, bf16[2560,256]{1,0:T(8,128)(2,1)} %edge_lat.1, bf16[320,256]{1,0:T(8,128)(2,1)} %node_ct.1, bf16[2560,256]{1,0:T(8,128)(2,1)} %edge_ct.1, ...), custom_call_target="tpu_custom_call" | custom-call | tf_op jit(solution)/shard_map/pallas_call | solution.py:496
  37.7 0.0 copy-start.3
  37.7 0.0 copy-start.1
  37.7 3.1 %convert_element_type.3 = f32[2560,256]{1,0:T(8,128)} convert(bf16[2560,256]{1,0:T(8,128)(2,1)} %get-tuple-element.11) | non-fusion elementwise | flops 655360 | bytes 3932160 | tf_op jit(solution)/shard_map/convert_element_type | solution.py:517
  40.8 0.0 copy-done.3
  40.8 0.7 %copy.26 = bf16[320,256]{1,0:T(8,128)(2,1)} copy(bf16[320,256]{1,0:T(8,128)(2,1)S(1)} %copy-done.3) | data formatting | bytes 327680
  41.5 0.0 copy-done.1
  41.5 0.0 copy-start.2
  41.5 1.1 %copy.27 = bf16[2560,256]{1,0:T(8,128)(2,1)} copy(bf16[2560,256]{1,0:T(8,128)(2,1)S(1)} %copy-done.1) | data formatting | bytes 2621440
  42.6 0.1 copy-done.2
  42.7 0.7 %copy.28 = f32[320,256]{1,0:T(8,128)} copy(f32[320,256]{1,0:T(8,128)S(1)} %copy-done.2) | data formatting | bytes 655360
  (1 shorter events, 0.0 us)
Async XLA Ops:
  0.6 0.8 %copy-start = (s32[8,8,80]{2,1,0:T(8,128)S(1)}, s32[8,8,80]{2,1,0:T(8,128)}, u32[]{:S(2)}) copy-start(s32[8,8,80]{2,1,0:T(8,128)} %param.21) | copy-start | bytes 61444
  37.7 3.1 %copy-start.3 = (bf16[320,256]{1,0:T(8,128)(2,1)S(1)}, bf16[320,256]{1,0:T(8,128)(2,1)}, u32[]{:S(2)}) copy-start(bf16[320,256]{1,0:T(8,128)(2,1)} %get-tuple-element.16) | copy-start | bytes 491524
  37.7 3.8 %copy-start.1 = (bf16[2560,256]{1,0:T(8,128)(2,1)S(1)}, bf16[2560,256]{1,0:T(8,128)(2,1)}, u32[]{:S(2)}) copy-start(bf16[2560,256]{1,0:T(8,128)(2,1)} %get-tuple-element.17) | copy-start | bytes 3932164
  41.5 1.2 %copy-start.2 = (f32[320,256]{1,0:T(8,128)S(1)}, f32[320,256]{1,0:T(8,128)}, u32[]{:S(2)}) copy-start(f32[320,256]{1,0:T(8,128)} %get-tuple-element.18) | copy-start | bytes 983044
